TPU v7x, 1024 devices: a whole 8x8x8 slice. The times are simulated.
1024 devices in a mesh: ax: 32 (over y_lo, x), circ: 32 (over z, y_hi, core).
Axes of the slice: x: 8, y: 8 (y_hi: 2, y_lo: 4; y = y_hi * 4 + y_lo), z: 8, core: 2. Of those that a mesh axis runs over, the one named last changes fastest.
Arguments:
- cotangent: float32 [16, 128, 4096], P(None, 'ax', 'circ'), may hold values from -6 to 6
- off_blocks: bfloat16 [8, 16, 16, 128, 4096], P(None, None, None, 'ax', 'circ'), may hold values from -0.375 to 0.375
- diag_inverse: bfloat16 [16, 16, 128, 4096], P(None, None, 'ax', 'circ'), may hold values from -1 to 1.6015625, as said below
Outputs:
- grad_source: float32 [16, 128, 4096], P(None, 'ax', 'circ')
- grad_initial: float32 [16, 128, 4096], P(None, 'ax', 'circ')
Inputs may be any that keep to these rules, and one draw needn't show every extreme that they name: `diag_inverse`: each cell's block has diagonal entries of 0.6 to about 1.6 and small signed entries elsewhere.
All inputs are finite; a program needn't handle non-finite values.
Results may differ from a plain program's by a relative error of at most 0.0003.
Values may be sent and summed in bfloat16 or wider, within the bound.
A program may use at most 64 MiB of HBM per device.

v0:
```python
import jax
import jax.numpy as jnp
from jax import lax
from jax.sharding import PartitionSpec as P

STEPS = 4


OFFSETS = ((-1, -1), (-1, 0), (-1, 1), (0, -1), (0, 1), (1, -1), (1, 0), (1, 1))


def extended_2(cells, sides, width, closed):
    for axis, dim in sides:
        count = lax.axis_size(axis)
        ends = count if closed else count - 1
        head = lax.slice_in_dim(cells, 0, width, axis=dim)
        tail = lax.slice_in_dim(cells, cells.shape[dim] - width, cells.shape[dim], axis=dim)
        cells = jnp.concatenate(
            [
                lax.ppermute(tail, axis, [(i, (i + 1) % count) for i in range(ends)]),
                cells,
                lax.ppermute(head, axis, [((i + 1) % count, i) for i in range(ends)]),
            ],
            axis=dim,
        )
    return cells


def block_products(blocks, weighted):
    return jnp.stack(
        [
            jnp.einsum(
                "rsac,rac->sac",
                blocks[slot].astype(jnp.float32),
                weighted,
                precision=lax.Precision.HIGHEST,
            )
            for slot in range(8)
        ]
    )


def collect(extended, rows, cols):
    total = jnp.zeros(extended.shape[1:2] + (rows, cols), jnp.float32)
    for slot in range(8):
        shift_a, shift_c = OFFSETS[slot]
        total = (
            total
            + extended[slot, :, 1 - shift_a : 1 - shift_a + rows, 1 - shift_c : 1 - shift_c + cols]
        )
    return total


def per_device(cotangent, off_blocks, diag_inverse):
    rows, cols = (cotangent.shape[1], cotangent.shape[2])
    adjoint = cotangent
    grad_source = jnp.zeros(cotangent.shape, jnp.float32)
    for step in range(STEPS):
        weighted = jnp.einsum(
            "rsac,rac->sac",
            diag_inverse.astype(jnp.float32),
            adjoint,
            precision=lax.Precision.HIGHEST,
        )
        grad_source = grad_source + weighted
        products = block_products(off_blocks, weighted)
        beside_all = extended_2(products, (("circ", 3),), 1, True)
        extended = extended_2(beside_all, (("ax", 2),), 1, False)
        adjoint = -collect(extended, rows, cols)
    return (grad_source, adjoint)


def solution(mesh):
    return jax.shard_map(
        per_device,
        mesh=mesh,
        in_specs=(
            P(None, "ax", "circ"),
            P(None, None, None, "ax", "circ"),
            P(None, None, "ax", "circ"),
        ),
        out_specs=(P(None, "ax", "circ"), P(None, "ax", "circ")),
        check_vma=False,
    )
```

profile of v0, /device:TPU:32, one launch (start us, length us, event | category | flops | bytes accessed | tf_op | source)
XLA Modules:
  0.0 148.8 jit_solution(5228970780665785554)
XLA Ops:
  0.6 1.1 fusion
  1.8 2.7 %fusion.32 = (f32[4,128,16]{1,0,2:T(4,128)S(1)}, f32[4,128,16]{1,0,2:T(4,128)S(1)}, f32[4,128,16]{1,0,2:T(4,128)S(1)}, f32[4,128,16]{1,0,2:T(4,128)S(1)}, f32[4,...) fusion(f32[4,128,16]{1,0,2:T(4,128)S(1)} %fusion, ...), kind=kLoop, calls=%fused_computation.68 | loop fusion | flops 3080192 | bytes 2392064
  4.8 2.1 %collective-permute-start = (f32[8,16,4,1]{3,1,2,0:T(8,128)S(1)}, f32[8,16,4,1]{3,1,2,0:T(8,128)S(1)}, u32[]{:S(2)}, u32[]{:S(2)}) collective-permute-start(f32[8,16,4,1]{3,1,2,0:T(8,128)S(1)} %get-tuple-element.48), channel_id=1, source_target_pairs={{0,1},{1,2},{2,3},{3,4},{4,5},{5,6},{6,7},{7,8},{8,9},{9,10},{10,1... | collective-permute-start | bytes 6152 | tf_op jit(solution)/shard_map/ppermute | solution.py:20
  6.8 20.7 %collective-permute-start.1 = (f32[8,16,4,1]{3,1,2,0:T(8,128)S(1)}, f32[8,16,4,1]{3,1,2,0:T(8,128)S(1)}, u32[]{:S(2)}, u32[]{:S(2)}) collective-permute-start(f32[8,16,4,1]{3,1,2,0:T(8,128)S(1)} %get-tuple-element.49), channel_id=1, source_target_pairs={{1,0},{2,1},{3,2},{4,3},{5,4},{6,5},{7,6},{8,7},{9,8},{10,9},{11,1... | collective-permute-start | bytes 6152 | tf_op jit(solution)/shard_map/ppermute | solution.py:22
  27.5 5.1 %collective-permute-done = f32[8,16,4,1]{3,1,2,0:T(8,128)S(1)} collective-permute-done((f32[8,16,4,1]{3,1,2,0:T(8,128)S(1)}, f32[8,16,4,1]{3,1,2,0:T(8,128)S(1)}, u32[]{:S(2)}, u32[]{:S(2)}) %collective-permute-start) | collective-permute-done | bytes 2080 | tf_op jit(solution)/shard_map/ppermute | solution.py:20
  32.6 1.6 %collective-permute-done.1 = f32[8,16,4,1]{3,1,2,0:T(8,128)S(1)} collective-permute-done((f32[8,16,4,1]{3,1,2,0:T(8,128)S(1)}, f32[8,16,4,1]{3,1,2,0:T(8,128)S(1)}, u32[]{:S(2)}, u32[]{:S(2)}) %collective-permute-start.1) | collective-permute-done | bytes 2080 | tf_op jit(solution)/shard_map/ppermute | solution.py:22
  34.3 6.9 %collective-permute-start.2 = (f32[8,16,1,130]{3,1,2,0:T(8,128)S(1)}, f32[8,16,1,130]{3,1,2,0:T(8,128)S(1)}, u32[]{:S(2)}, u32[]{:S(2)}) collective-permute-start(f32[8,16,1,130]{3,1,2,0:T(8,128)S(1)} %get-tuple-element.40), channel_id=1, source_target_pairs={{32,0},{64,32},{96,64},{128,96},{160,128},{192,160},{224,192},{256... | collective-permute-start | bytes 199688 | tf_op jit(solution)/shard_map/ppermute | solution.py:22
  41.2 1.9 %collective-permute-start.3 = (f32[8,16,1,130]{3,1,2,0:T(8,128)S(1)}, f32[8,16,1,130]{3,1,2,0:T(8,128)S(1)}, u32[]{:S(2)}, u32[]{:S(2)}) collective-permute-start(f32[8,16,1,130]{3,1,2,0:T(8,128)S(1)} %get-tuple-element.41), channel_id=1, source_target_pairs={{0,32},{32,64},{64,96},{96,128},{128,160},{160,192},{192,224},{224... | collective-permute-start | bytes 199688 | tf_op jit(solution)/shard_map/ppermute | solution.py:20
  43.7 6.5 %collective-permute-done.3 = f32[8,16,1,130]{3,1,2,0:T(8,128)S(1)} collective-permute-done((f32[8,16,1,130]{3,1,2,0:T(8,128)S(1)}, f32[8,16,1,130]{3,1,2,0:T(8,128)S(1)}, u32[]{:S(2)}, u32[]{:S(2)}) %collective-permute-start.3) | collective-permute-done | bytes 66592 | tf_op jit(solution)/shard_map/ppermute | solution.py:20
  50.6 1.2 fusion.33
  52.0 1.9 %collective-permute-start.4 = (f32[8,16,4,1]{3,1,2,0:T(8,128)S(1)}, f32[8,16,4,1]{3,1,2,0:T(8,128)S(1)}, u32[]{:S(2)}, u32[]{:S(2)}) collective-permute-start(f32[8,16,4,1]{3,1,2,0:T(8,128)S(1)} %get-tuple-element.46), channel_id=1, source_target_pairs={{0,1},{1,2},{2,3},{3,4},{4,5},{5,6},{6,7},{7,8},{8,9},{9,10},{10,1... | collective-permute-start | bytes 6152 | tf_op jit(solution)/shard_map/ppermute | solution.py:20
  53.9 10.7 %collective-permute-start.5 = (f32[8,16,4,1]{3,1,2,0:T(8,128)S(1)}, f32[8,16,4,1]{3,1,2,0:T(8,128)S(1)}, u32[]{:S(2)}, u32[]{:S(2)}) collective-permute-start(f32[8,16,4,1]{3,1,2,0:T(8,128)S(1)} %get-tuple-element.47), channel_id=1, source_target_pairs={{1,0},{2,1},{3,2},{4,3},{5,4},{6,5},{7,6},{8,7},{9,8},{10,9},{11,1... | collective-permute-start | bytes 6152 | tf_op jit(solution)/shard_map/ppermute | solution.py:22
  64.6 3.5 %collective-permute-done.4 = f32[8,16,4,1]{3,1,2,0:T(8,128)S(1)} collective-permute-done((f32[8,16,4,1]{3,1,2,0:T(8,128)S(1)}, f32[8,16,4,1]{3,1,2,0:T(8,128)S(1)}, u32[]{:S(2)}, u32[]{:S(2)}) %collective-permute-start.4) | collective-permute-done | bytes 2080 | tf_op jit(solution)/shard_map/ppermute | solution.py:20
  68.1 4.0 %collective-permute-done.5 = f32[8,16,4,1]{3,1,2,0:T(8,128)S(1)} collective-permute-done((f32[8,16,4,1]{3,1,2,0:T(8,128)S(1)}, f32[8,16,4,1]{3,1,2,0:T(8,128)S(1)}, u32[]{:S(2)}, u32[]{:S(2)}) %collective-permute-start.5) | collective-permute-done | bytes 2080 | tf_op jit(solution)/shard_map/ppermute | solution.py:22
  72.2 1.9 %collective-permute-start.6 = (f32[8,16,1,130]{3,1,2,0:T(8,128)S(1)}, f32[8,16,1,130]{3,1,2,0:T(8,128)S(1)}, u32[]{:S(2)}, u32[]{:S(2)}) collective-permute-start(f32[8,16,1,130]{3,1,2,0:T(8,128)S(1)} %get-tuple-element.38), channel_id=1, source_target_pairs={{32,0},{64,32},{96,64},{128,96},{160,128},{192,160},{224,192},{256... | collective-permute-start | bytes 199688 | tf_op jit(solution)/shard_map/ppermute | solution.py:22
  74.2 3.9 %collective-permute-start.7 = (f32[8,16,1,130]{3,1,2,0:T(8,128)S(1)}, f32[8,16,1,130]{3,1,2,0:T(8,128)S(1)}, u32[]{:S(2)}, u32[]{:S(2)}) collective-permute-start(f32[8,16,1,130]{3,1,2,0:T(8,128)S(1)} %get-tuple-element.39), channel_id=1, source_target_pairs={{0,32},{32,64},{64,96},{96,128},{128,160},{160,192},{192,224},{224... | collective-permute-start | bytes 199688 | tf_op jit(solution)/shard_map/ppermute | solution.py:20
  79.1 4.4 %collective-permute-done.7 = f32[8,16,1,130]{3,1,2,0:T(8,128)S(1)} collective-permute-done((f32[8,16,1,130]{3,1,2,0:T(8,128)S(1)}, f32[8,16,1,130]{3,1,2,0:T(8,128)S(1)}, u32[]{:S(2)}, u32[]{:S(2)}) %collective-permute-start.7) | collective-permute-done | bytes 66592 | tf_op jit(solution)/shard_map/ppermute | solution.py:20
  83.9 1.2 fusion.34
  85.3 1.9 %collective-permute-start.8 = (f32[8,16,4,1]{3,1,2,0:T(8,128)S(1)}, f32[8,16,4,1]{3,1,2,0:T(8,128)S(1)}, u32[]{:S(2)}, u32[]{:S(2)}) collective-permute-start(f32[8,16,4,1]{3,1,2,0:T(8,128)S(1)} %get-tuple-element.44), channel_id=1, source_target_pairs={{0,1},{1,2},{2,3},{3,4},{4,5},{5,6},{6,7},{7,8},{8,9},{9,10},{10,1... | collective-permute-start | bytes 6152 | tf_op jit(solution)/shard_map/ppermute | solution.py:20
  87.3 12.1 %collective-permute-start.9 = (f32[8,16,4,1]{3,1,2,0:T(8,128)S(1)}, f32[8,16,4,1]{3,1,2,0:T(8,128)S(1)}, u32[]{:S(2)}, u32[]{:S(2)}) collective-permute-start(f32[8,16,4,1]{3,1,2,0:T(8,128)S(1)} %get-tuple-element.45), channel_id=1, source_target_pairs={{1,0},{2,1},{3,2},{4,3},{5,4},{6,5},{7,6},{8,7},{9,8},{10,9},{11,1... | collective-permute-start | bytes 6152 | tf_op jit(solution)/shard_map/ppermute | solution.py:22
  99.3 2.2 %collective-permute-done.8 = f32[8,16,4,1]{3,1,2,0:T(8,128)S(1)} collective-permute-done((f32[8,16,4,1]{3,1,2,0:T(8,128)S(1)}, f32[8,16,4,1]{3,1,2,0:T(8,128)S(1)}, u32[]{:S(2)}, u32[]{:S(2)}) %collective-permute-start.8) | collective-permute-done | bytes 2080 | tf_op jit(solution)/shard_map/ppermute | solution.py:20
  101.6 1.9 %collective-permute-done.9 = f32[8,16,4,1]{3,1,2,0:T(8,128)S(1)} collective-permute-done((f32[8,16,4,1]{3,1,2,0:T(8,128)S(1)}, f32[8,16,4,1]{3,1,2,0:T(8,128)S(1)}, u32[]{:S(2)}, u32[]{:S(2)}) %collective-permute-start.9) | collective-permute-done | bytes 2080 | tf_op jit(solution)/shard_map/ppermute | solution.py:22
  103.7 4.0 %collective-permute-start.10 = (f32[8,16,1,130]{3,1,2,0:T(8,128)S(1)}, f32[8,16,1,130]{3,1,2,0:T(8,128)S(1)}, u32[]{:S(2)}, u32[]{:S(2)}) collective-permute-start(f32[8,16,1,130]{3,1,2,0:T(8,128)S(1)} %get-tuple-element.36), channel_id=1, source_target_pairs={{32,0},{64,32},{96,64},{128,96},{160,128},{192,160},{224,192},{256... | collective-permute-start | bytes 199688 | tf_op jit(solution)/shard_map/ppermute | solution.py:22
  107.7 1.9 %collective-permute-start.11 = (f32[8,16,1,130]{3,1,2,0:T(8,128)S(1)}, f32[8,16,1,130]{3,1,2,0:T(8,128)S(1)}, u32[]{:S(2)}, u32[]{:S(2)}) collective-permute-start(f32[8,16,1,130]{3,1,2,0:T(8,128)S(1)} %get-tuple-element.37), channel_id=1, source_target_pairs={{0,32},{32,64},{64,96},{96,128},{128,160},{160,192},{192,224},{224... | collective-permute-start | bytes 199688 | tf_op jit(solution)/shard_map/ppermute | solution.py:20
  110.5 7.4 %collective-permute-done.11 = f32[8,16,1,130]{3,1,2,0:T(8,128)S(1)} collective-permute-done((f32[8,16,1,130]{3,1,2,0:T(8,128)S(1)}, f32[8,16,1,130]{3,1,2,0:T(8,128)S(1)}, u32[]{:S(2)}, u32[]{:S(2)}) %collective-permute-start.11) | collective-permute-done | bytes 66592 | tf_op jit(solution)/shard_map/ppermute | solution.py:20
  118.3 1.2 fusion.35
  119.8 1.9 %collective-permute-start.12 = (f32[8,16,4,1]{3,2,1,0:T(4,128)S(1)}, f32[8,16,4,1]{3,2,1,0:T(4,128)S(1)}, u32[]{:S(2)}, u32[]{:S(2)}) collective-permute-start(f32[8,16,4,1]{3,2,1,0:T(4,128)S(1)} %get-tuple-element.42), channel_id=1, source_target_pairs={{0,1},{1,2},{2,3},{3,4},{4,5},{5,6},{6,7},{7,8},{8,9},{9,10},{10,1... | collective-permute-start | bytes 6152 | tf_op jit(solution)/shard_map/ppermute | solution.py:20
  121.8 9.7 %collective-permute-start.13 = (f32[8,16,4,1]{3,2,1,0:T(4,128)S(1)}, f32[8,16,4,1]{3,2,1,0:T(4,128)S(1)}, u32[]{:S(2)}, u32[]{:S(2)}) collective-permute-start(f32[8,16,4,1]{3,2,1,0:T(4,128)S(1)} %get-tuple-element.43), channel_id=1, source_target_pairs={{1,0},{2,1},{3,2},{4,3},{5,4},{6,5},{7,6},{8,7},{9,8},{10,9},{11,1... | collective-permute-start | bytes 6152 | tf_op jit(solution)/shard_map/ppermute | solution.py:22
  131.4 4.6 %collective-permute-done.12 = f32[8,16,4,1]{3,2,1,0:T(4,128)S(1)} collective-permute-done((f32[8,16,4,1]{3,2,1,0:T(4,128)S(1)}, f32[8,16,4,1]{3,2,1,0:T(4,128)S(1)}, u32[]{:S(2)}, u32[]{:S(2)}) %collective-permute-start.12) | collective-permute-done | bytes 2080 | tf_op jit(solution)/shard_map/ppermute | solution.py:20
  136.9 1.9 %collective-permute-start.14 = (f32[8,16,1,130]{3,2,1,0:T(1,128)S(1)}, f32[8,16,1,130]{3,2,1,0:T(1,128)S(1)}, u32[]{:S(2)}, u32[]{:S(2)}) collective-permute-start(f32[8,16,1,130]{3,2,1,0:T(1,128)S(1)} %get-tuple-element.34), channel_id=1, source_target_pairs={{32,0},{64,32},{96,64},{128,96},{160,128},{192,160},{224,192},{256... | collective-permute-start | bytes 199688 | tf_op jit(solution)/shard_map/ppermute | solution.py:22
  138.8 3.9 %collective-permute-start.15 = (f32[8,16,1,130]{3,2,1,0:T(1,128)S(1)}, f32[8,16,1,130]{3,2,1,0:T(1,128)S(1)}, u32[]{:S(2)}, u32[]{:S(2)}) collective-permute-start(f32[8,16,1,130]{3,2,1,0:T(1,128)S(1)} %get-tuple-element.35), channel_id=1, source_target_pairs={{0,32},{32,64},{64,96},{96,128},{128,160},{160,192},{192,224},{224... | collective-permute-start | bytes 199688 | tf_op jit(solution)/shard_map/ppermute | solution.py:20
  143.8 4.0 %collective-permute-done.15 = f32[8,16,1,130]{3,2,1,0:T(1,128)S(1)} collective-permute-done((f32[8,16,1,130]{3,2,1,0:T(1,128)S(1)}, f32[8,16,1,130]{3,2,1,0:T(1,128)S(1)}, u32[]{:S(2)}, u32[]{:S(2)}) %collective-permute-start.15) | collective-permute-done | bytes 66592 | tf_op jit(solution)/shard_map/ppermute | solution.py:20
  (60 shorter events, 7.7 us)
Async XLA Ops:
  4.5 45.9 %copy-start.1 = (bf16[16,16,4,128]{3,2,1,0:T(4,128)(2,1)S(1)}, bf16[16,16,4,128]{3,2,1,0:T(4,128)(2,1)}, u32[]{:S(2)}) copy-start(bf16[16,16,4,128]{3,2,1,0:T(4,128)(2,1)} %param.5) | copy-start | bytes 786436
  4.5 46.0 %copy-start = (bf16[8,16,16,4,128]{4,3,2,1,0:T(4,128)(2,1)S(1)}, bf16[8,16,16,4,128]{4,3,2,1,0:T(4,128)(2,1)}, u32[]{:S(2)}) copy-start(bf16[8,16,16,4,128]{4,3,2,1,0:T(4,128)(2,1)} %param.4) | copy-start | bytes 6291460
  4.8 27.8 %collective-permute-start = (f32[8,16,4,1]{3,1,2,0:T(8,128)S(1)}, f32[8,16,4,1]{3,1,2,0:T(8,128)S(1)}, u32[]{:S(2)}, u32[]{:S(2)}) collective-permute-start(f32[8,16,4,1]{3,1,2,0:T(8,128)S(1)} %get-tuple-element.48), channel_id=1, source_target_pairs={{0,1},{1,2},{2,3},{3,4},{4,5},{5,6},{6,7},{7,8},{8,9},{9,10},{10,1... | collective-permute-start | bytes 6152 | tf_op jit(solution)/shard_map/ppermute | solution.py:20
  6.8 27.4 %collective-permute-start.1 = (f32[8,16,4,1]{3,1,2,0:T(8,128)S(1)}, f32[8,16,4,1]{3,1,2,0:T(8,128)S(1)}, u32[]{:S(2)}, u32[]{:S(2)}) collective-permute-start(f32[8,16,4,1]{3,1,2,0:T(8,128)S(1)} %get-tuple-element.49), channel_id=1, source_target_pairs={{1,0},{2,1},{3,2},{4,3},{5,4},{6,5},{7,6},{8,7},{9,8},{10,9},{11,1... | collective-permute-start | bytes 6152 | tf_op jit(solution)/shard_map/ppermute | solution.py:22
  34.3 9.4 %collective-permute-start.2 = (f32[8,16,1,130]{3,1,2,0:T(8,128)S(1)}, f32[8,16,1,130]{3,1,2,0:T(8,128)S(1)}, u32[]{:S(2)}, u32[]{:S(2)}) collective-permute-start(f32[8,16,1,130]{3,1,2,0:T(8,128)S(1)} %get-tuple-element.40), channel_id=1, source_target_pairs={{32,0},{64,32},{96,64},{128,96},{160,128},{192,160},{224,192},{256... | collective-permute-start | bytes 199688 | tf_op jit(solution)/shard_map/ppermute | solution.py:22
  41.2 9.0 %collective-permute-start.3 = (f32[8,16,1,130]{3,1,2,0:T(8,128)S(1)}, f32[8,16,1,130]{3,1,2,0:T(8,128)S(1)}, u32[]{:S(2)}, u32[]{:S(2)}) collective-permute-start(f32[8,16,1,130]{3,1,2,0:T(8,128)S(1)} %get-tuple-element.41), channel_id=1, source_target_pairs={{0,32},{32,64},{64,96},{96,128},{128,160},{160,192},{192,224},{224... | collective-permute-start | bytes 199688 | tf_op jit(solution)/shard_map/ppermute | solution.py:20
  52.0 16.1 %collective-permute-start.4 = (f32[8,16,4,1]{3,1,2,0:T(8,128)S(1)}, f32[8,16,4,1]{3,1,2,0:T(8,128)S(1)}, u32[]{:S(2)}, u32[]{:S(2)}) collective-permute-start(f32[8,16,4,1]{3,1,2,0:T(8,128)S(1)} %get-tuple-element.46), channel_id=1, source_target_pairs={{0,1},{1,2},{2,3},{3,4},{4,5},{5,6},{6,7},{7,8},{8,9},{9,10},{10,1... | collective-permute-start | bytes 6152 | tf_op jit(solution)/shard_map/ppermute | solution.py:20
  53.9 18.2 %collective-permute-start.5 = (f32[8,16,4,1]{3,1,2,0:T(8,128)S(1)}, f32[8,16,4,1]{3,1,2,0:T(8,128)S(1)}, u32[]{:S(2)}, u32[]{:S(2)}) collective-permute-start(f32[8,16,4,1]{3,1,2,0:T(8,128)S(1)} %get-tuple-element.47), channel_id=1, source_target_pairs={{1,0},{2,1},{3,2},{4,3},{5,4},{6,5},{7,6},{8,7},{9,8},{10,9},{11,1... | collective-permute-start | bytes 6152 | tf_op jit(solution)/shard_map/ppermute | solution.py:22
  72.2 6.9 %collective-permute-start.6 = (f32[8,16,1,130]{3,1,2,0:T(8,128)S(1)}, f32[8,16,1,130]{3,1,2,0:T(8,128)S(1)}, u32[]{:S(2)}, u32[]{:S(2)}) collective-permute-start(f32[8,16,1,130]{3,1,2,0:T(8,128)S(1)} %get-tuple-element.38), channel_id=1, source_target_pairs={{32,0},{64,32},{96,64},{128,96},{160,128},{192,160},{224,192},{256... | collective-permute-start | bytes 199688 | tf_op jit(solution)/shard_map/ppermute | solution.py:22
  74.2 9.4 %collective-permute-start.7 = (f32[8,16,1,130]{3,1,2,0:T(8,128)S(1)}, f32[8,16,1,130]{3,1,2,0:T(8,128)S(1)}, u32[]{:S(2)}, u32[]{:S(2)}) collective-permute-start(f32[8,16,1,130]{3,1,2,0:T(8,128)S(1)} %get-tuple-element.39), channel_id=1, source_target_pairs={{0,32},{32,64},{64,96},{96,128},{128,160},{160,192},{192,224},{224... | collective-permute-start | bytes 199688 | tf_op jit(solution)/shard_map/ppermute | solution.py:20
  85.3 16.3 %collective-permute-start.8 = (f32[8,16,4,1]{3,1,2,0:T(8,128)S(1)}, f32[8,16,4,1]{3,1,2,0:T(8,128)S(1)}, u32[]{:S(2)}, u32[]{:S(2)}) collective-permute-start(f32[8,16,4,1]{3,1,2,0:T(8,128)S(1)} %get-tuple-element.44), channel_id=1, source_target_pairs={{0,1},{1,2},{2,3},{3,4},{4,5},{5,6},{6,7},{7,8},{8,9},{9,10},{10,1... | collective-permute-start | bytes 6152 | tf_op jit(solution)/shard_map/ppermute | solution.py:20
  87.3 16.3 %collective-permute-start.9 = (f32[8,16,4,1]{3,1,2,0:T(8,128)S(1)}, f32[8,16,4,1]{3,1,2,0:T(8,128)S(1)}, u32[]{:S(2)}, u32[]{:S(2)}) collective-permute-start(f32[8,16,4,1]{3,1,2,0:T(8,128)S(1)} %get-tuple-element.45), channel_id=1, source_target_pairs={{1,0},{2,1},{3,2},{4,3},{5,4},{6,5},{7,6},{8,7},{9,8},{10,9},{11,1... | collective-permute-start | bytes 6152 | tf_op jit(solution)/shard_map/ppermute | solution.py:22
  103.7 6.9 %collective-permute-start.10 = (f32[8,16,1,130]{3,1,2,0:T(8,128)S(1)}, f32[8,16,1,130]{3,1,2,0:T(8,128)S(1)}, u32[]{:S(2)}, u32[]{:S(2)}) collective-permute-start(f32[8,16,1,130]{3,1,2,0:T(8,128)S(1)} %get-tuple-element.36), channel_id=1, source_target_pairs={{32,0},{64,32},{96,64},{128,96},{160,128},{192,160},{224,192},{256... | collective-permute-start | bytes 199688 | tf_op jit(solution)/shard_map/ppermute | solution.py:22
  107.7 10.3 %collective-permute-start.11 = (f32[8,16,1,130]{3,1,2,0:T(8,128)S(1)}, f32[8,16,1,130]{3,1,2,0:T(8,128)S(1)}, u32[]{:S(2)}, u32[]{:S(2)}) collective-permute-start(f32[8,16,1,130]{3,1,2,0:T(8,128)S(1)} %get-tuple-element.37), channel_id=1, source_target_pairs={{0,32},{32,64},{64,96},{96,128},{128,160},{160,192},{192,224},{224... | collective-permute-start | bytes 199688 | tf_op jit(solution)/shard_map/ppermute | solution.py:20
  119.8 16.2 %collective-permute-start.12 = (f32[8,16,4,1]{3,2,1,0:T(4,128)S(1)}, f32[8,16,4,1]{3,2,1,0:T(4,128)S(1)}, u32[]{:S(2)}, u32[]{:S(2)}) collective-permute-start(f32[8,16,4,1]{3,2,1,0:T(4,128)S(1)} %get-tuple-element.42), channel_id=1, source_target_pairs={{0,1},{1,2},{2,3},{3,4},{4,5},{5,6},{6,7},{7,8},{8,9},{9,10},{10,1... | collective-permute-start | bytes 6152 | tf_op jit(solution)/shard_map/ppermute | solution.py:20
  121.8 14.3 %collective-permute-start.13 = (f32[8,16,4,1]{3,2,1,0:T(4,128)S(1)}, f32[8,16,4,1]{3,2,1,0:T(4,128)S(1)}, u32[]{:S(2)}, u32[]{:S(2)}) collective-permute-start(f32[8,16,4,1]{3,2,1,0:T(4,128)S(1)} %get-tuple-element.43), channel_id=1, source_target_pairs={{1,0},{2,1},{3,2},{4,3},{5,4},{6,5},{7,6},{8,7},{9,8},{10,9},{11,1... | collective-permute-start | bytes 6152 | tf_op jit(solution)/shard_map/ppermute | solution.py:22
  136.9 6.9 %collective-permute-start.14 = (f32[8,16,1,130]{3,2,1,0:T(1,128)S(1)}, f32[8,16,1,130]{3,2,1,0:T(1,128)S(1)}, u32[]{:S(2)}, u32[]{:S(2)}) collective-permute-start(f32[8,16,1,130]{3,2,1,0:T(1,128)S(1)} %get-tuple-element.34), channel_id=1, source_target_pairs={{32,0},{64,32},{96,64},{128,96},{160,128},{192,160},{224,192},{256... | collective-permute-start | bytes 199688 | tf_op jit(solution)/shard_map/ppermute | solution.py:22
  138.8 9.0 %collective-permute-start.15 = (f32[8,16,1,130]{3,2,1,0:T(1,128)S(1)}, f32[8,16,1,130]{3,2,1,0:T(1,128)S(1)}, u32[]{:S(2)}, u32[]{:S(2)}) collective-permute-start(f32[8,16,1,130]{3,2,1,0:T(1,128)S(1)} %get-tuple-element.35), channel_id=1, source_target_pairs={{0,32},{32,64},{64,96},{96,128},{128,160},{160,192},{192,224},{224... | collective-permute-start | bytes 199688 | tf_op jit(solution)/shard_map/ppermute | solution.py:20
where the time goes:
time: 149 us
  starting transfers between devices  87.3 us (59%)
  waiting for transfers between devices  48.2 us (32%)
  other arithmetic  11.4 us (8%)
    ppermute x8, starting transfers between devices, extended_2(): lax.ppermute(head, axis, [((i + 1) % count, i) for i in range(ends)])  67.8 us
    ppermute x8, waiting for transfers between devices, extended_2(): lax.ppermute(tail, axis, [(i, (i + 1) % count) for i in range(ends)])  37.8 us
    ppermute x8, starting transfers between devices, extended_2(): lax.ppermute(tail, axis, [(i, (i + 1) % count) for i in range(ends)])  19.5 us
    ppermute x8, waiting for transfers between devices, extended_2(): lax.ppermute(head, axis, [((i + 1) % count, i) for i in range(ends)])  10.4 us
    unnamed x6, other arithmetic  5.6 us
  transfers between devices with their start and end apart: 16, of which 15 were waited for; matrix products, arithmetic and copies ran while one was open for 0% of the time, Pallas kernels for 0%

commit v1 on v0

v1 whole, which is shorter than its diff:
```python
import functools

import jax
import jax.numpy as jnp
from jax import lax
from jax.experimental import pallas as pl
from jax.experimental.pallas import tpu as pltpu
from jax.sharding import PartitionSpec as P

STEPS = 4
MESH = pl.DeviceIdType.MESH
F32 = jnp.float32
BF16 = jnp.bfloat16


def halves(field):
    sub = lax.broadcasted_iota(jnp.int32, (8, 128), 0)
    out = []
    for v in range(8):
        here = field[8 * v : 8 * v + 8]
        turned = pltpu.roll(here, 4, 0)
        out.append(jnp.where(sub < 4, here, turned))
        out.append(jnp.where(sub < 4, turned, here))
    return out


def spread(field):
    sub = lax.broadcasted_iota(jnp.int32, (8, 128), 0)
    group = lax.broadcasted_iota(jnp.int32, (8, 128), 1) >> 3
    total = jnp.zeros((8, 128), F32)
    for v in range(8):
        total = jnp.where(group == 2 * v + (sub >> 2), field[8 * v : 8 * v + 8], total)
    return total + pltpu.roll(total, 4, 0)


def split(x, parts):
    out = []
    for _ in range(parts):
        part = x.astype(BF16)
        out.append(part)
        x = x - part.astype(F32)
    return out


def times(blocks, rows):
    return (blocks.reshape(8, 8, 128) * rows[None]).reshape(64, 128)


def kernel(
    cot,
    off,
    diag,
    source_out,
    initial_out,
    av,
    bv,
    dv,
    source,
    ghost_b,
    ghost_d,
    out_b,
    in_b,
    out_a,
    in_a,
    pk,
    up_s,
    down_s,
    q,
    ax_out,
    ax_in,
    pick,
    same,
    moves,
    load_sem,
    store_sem,
    gsend,
    grecv,
    asend,
    arecv,
):
    ax, circ = lax.axis_index("ax"), lax.axis_index("circ")
    n_ax, n_circ = lax.axis_size("ax"), lax.axis_size("circ")
    right = (ax, lax.rem(circ + 1, n_circ))
    left = (ax, lax.rem(circ + n_circ - 1, n_circ))
    above, below = (ax - 1, circ), (ax + 1, circ)
    has_above, has_below = ax > 0, ax < n_ax - 1

    loads = [
        pltpu.make_async_copy(cot, av, load_sem.at[8]),
        pltpu.make_async_copy(diag, dv, load_sem.at[9]),
    ]
    for copy in loads:
        copy.start()

    def load(k):
        return pltpu.make_async_copy(off.at[k], bv.at[k], load_sem.at[k])

    for k in range(8):
        load(k).start()

    @pl.when(jnp.logical_not(has_above))
    def _():
        ax_in[:, 0] = jnp.zeros((STEPS, 32, 128), F32)

    @pl.when(jnp.logical_not(has_below))
    def _():
        ax_in[:, 1] = jnp.zeros((STEPS, 32, 128), F32)

    barrier = pltpu.get_barrier_semaphore()
    pl.semaphore_signal(barrier, inc=1, device_id=right, device_id_type=MESH)
    pl.semaphore_signal(barrier, inc=1, device_id=left, device_id_type=MESH)

    @pl.when(has_above)
    def _():
        pl.semaphore_signal(barrier, inc=1, device_id=above, device_id_type=MESH)

    @pl.when(has_below)
    def _():
        pl.semaphore_signal(barrier, inc=1, device_id=below, device_id_type=MESH)

    row = lax.broadcasted_iota(jnp.int32, (256, 128), 0)
    col = lax.broadcasted_iota(jnp.int32, (256, 128), 1)
    edge = ((row + 4) & 127) == (col & 7)
    pick[...] = jnp.where(edge & (((col >> 3) & 1) == (row >> 7)), 1.0, 0.0).astype(BF16)
    same[0] = jnp.where((row & 7) == (col & 7), 1.0, 0.0).astype(BF16)
    same[1] = jnp.where(edge, 1.0, 0.0).astype(BF16)
    g_from, g_to = row & 7, col & 7
    for i, shift in enumerate((-1, 0, 1)):
        inside = g_to == g_from + shift
        if shift == 1:
            inside = inside & (g_from != 3)
            outside = (g_from == 3) & (col == 0)
        elif shift == -1:
            inside = inside & (g_from != 4)
            outside = (g_from == 4) & (col == 127)
        moves[i, :, 128:] = jnp.where(inside, 1.0, 0.0).astype(BF16)
        if shift == 0:
            moves[i, :, :128] = jnp.zeros((256, 128), BF16)
        else:
            moves[i, :, :128] = jnp.where(outside, 1.0, 0.0).astype(BF16)

    lane = lax.broadcasted_iota(jnp.int32, (64, 128), 1)
    sub = lax.broadcasted_iota(jnp.int32, (64, 128), 0)
    ghost = lane & 7

    def pick_edges(blocks):
        both = jnp.concatenate(
            [blocks[:, 0].reshape(512, 128), blocks[:, 1].reshape(512, 128)], axis=1
        )
        found = jnp.dot(both, pick[...], preferred_element_type=F32)
        total = found[0:64]
        for p in range(1, 8):
            total = jnp.where((lane >> 4) == p, found[64 * p : 64 * p + 64], total)
        return total

    loads[0].wait()
    field = av[...]
    copies = [
        jnp.dot(part, same[1, :128], preferred_element_type=F32) for part in split(field, 3)
    ]
    out_a[...] = spread(copies[0] + copies[1] + copies[2])
    loads[1].wait()
    edges = pick_edges(dv[...]).astype(BF16)
    out_b[0, 4] = edges
    out_b[1, 4] = edges

    @pl.loop(0, 4)
    def _(pair):
        load(2 * pair).wait()
        first = pick_edges(bv[2 * pair])
        load(2 * pair + 1).wait()
        second = pick_edges(bv[2 * pair + 1])
        out_b[0, pair] = jnp.where(ghost < 4, first, pltpu.roll(second, 4, 1)).astype(BF16)
        out_b[1, pair] = jnp.where(ghost < 4, pltpu.roll(first, 124, 1), second).astype(BF16)

    pl.semaphore_wait(
        barrier, 2 + has_above.astype(jnp.int32) + has_below.astype(jnp.int32)
    )

    ghosts = []
    for side, target in ((0, right), (1, left)):
        ghosts.append(
            pltpu.make_async_remote_copy(
                src_ref=out_b.at[side],
                dst_ref=in_b.at[side],
                send_sem=gsend.at[side],
                recv_sem=grecv.at[side],
                device_id=target,
                device_id_type=MESH,
            )
        )
        ghosts.append(
            pltpu.make_async_remote_copy(
                src_ref=out_a,
                dst_ref=in_a.at[side],
                send_sem=gsend.at[2 + side],
                recv_sem=grecv.at[2 + side],
                device_id=target,
                device_id_type=MESH,
            )
        )
    for copy in ghosts:
        copy.start()

    def weigh(a, first):
        rows = halves(a)
        w = jnp.zeros((64, 128), F32)
        for r in range(16):
            w = w + times(dv[r // 2, r % 2].astype(F32), rows[r])
        source[...] = w if first else source[...] + w
        return w

    def products(w):
        rows = halves(w)

        @pl.loop(0, 8)
        def _(k):
            total = jnp.zeros((64, 128), F32)
            for r in range(16):
                total = total + times(bv[k, r // 2, r % 2].astype(F32), rows[r])
            pk[k] = total

    def message(step, way, target):
        return pltpu.make_async_remote_copy(
            src_ref=ax_out.at[step, way],
            dst_ref=ax_in.at[step, way],
            send_sem=asend.at[step, way],
            recv_sem=arecv.at[step, way],
            device_id=target,
            device_id_type=MESH,
        )

    products(weigh(field, True))

    for copy in ghosts:
        copy.wait_recv()
    lane8 = lax.broadcasted_iota(jnp.int32, (8, 128), 1)
    ghost_a = jnp.where((lane8 & 7) < 4, in_a[0], in_a[1])
    ghost_d[...] = jnp.where(ghost < 4, in_b[0, 4].astype(F32), in_b[1, 4].astype(F32))

    @pl.loop(0, 4)
    def _(pair):
        from_left = in_b[0, pair].astype(F32)
        from_right = in_b[1, pair].astype(F32)
        ghost_b[2 * pair] = jnp.where(ghost < 4, from_left, pltpu.roll(from_right, 4, 1))
        ghost_b[2 * pair + 1] = jnp.where(ghost < 4, pltpu.roll(from_left, 124, 1), from_right)

    for step in range(STEPS):
        if step > 0:
            a = -q[0:64]
            ghost_a = spread(-q[64:128])
            products(weigh(a, False))
        if step == STEPS - 1:
            pltpu.make_async_copy(source, source_out, store_sem.at[0]).start()

        ghost_w = jnp.dot(
            jnp.concatenate(split(times(ghost_d[...], ghost_a), 2), axis=1),
            same[0],
            preferred_element_type=F32,
        )
        rows = spread(ghost_w)
        moved = []
        for i, slots in enumerate(((0, 3, 5), (1, 6), (2, 4, 7))):
            p = jnp.concatenate([times(ghost_b[k], rows) for k in slots], axis=0)
            moved.append(
                jnp.dot(
                    jnp.concatenate(split(p, 2), axis=1), moves[i], preferred_element_type=F32
                )
            )
        from_ghosts = (
            moved[0][0:64] + moved[1][0:64] + moved[2][0:64],
            moved[0][64:128] + moved[2][64:128],
            moved[0][128:192] + moved[1][64:128] + moved[2][128:192],
        )

        def gathered(way, slot_left, slot_same, slot_right):
            to_left, to_right = pk[slot_left], pk[slot_right]
            main = jnp.where(lane == 127, 0.0, pltpu.roll(to_left, 127, 1))
            main = main + jnp.where(lane == 0, 0.0, pltpu.roll(to_right, 1, 1))
            if slot_same is not None:
                main = main + pk[slot_same]
            main = main + from_ghosts[way][:, :128]
            beyond = jnp.where(ghost == 3, to_left[:, 0:1], 0.0)
            beyond = jnp.where(ghost == 4, to_right[:, 127:128], beyond)
            beyond = beyond + from_ghosts[way][:, 128:]
            return main, beyond

        up = gathered(0, 0, 1, 2)
        up_s[0:64] = up[0]
        up_s[64:128] = up[1]
        down = gathered(2, 5, 6, 7)
        down_s[0:64] = down[0]
        down_s[64:128] = down[1]
        ax_out[step, 1] = up_s[pl.ds(0, 32, stride=4)]
        ax_out[step, 0] = down_s[pl.ds(3, 32, stride=4)]

        @pl.when(has_above)
        def _():
            message(step, 1, above).start()

        @pl.when(has_below)
        def _():
            message(step, 0, below).start()

        middle = gathered(1, 3, None, 4)
        for part in range(2):
            lifted = pltpu.roll(up[part].reshape(8, 8, 128), 7, 1).reshape(64, 128)
            dropped = pltpu.roll(down[part].reshape(8, 8, 128), 1, 1).reshape(64, 128)
            q[64 * part : 64 * part + 64] = (
                middle[part]
                + jnp.where((sub & 3) == 3, 0.0, lifted)
                + jnp.where((sub & 3) == 0, 0.0, dropped)
            )

        @pl.when(has_above)
        def _():
            message(step, 0, above).wait_recv()

        @pl.when(has_below)
        def _():
            message(step, 1, below).wait_recv()

        q[pl.ds(0, 32, stride=4)] = q[pl.ds(0, 32, stride=4)] + ax_in[step, 0]
        q[pl.ds(3, 32, stride=4)] = q[pl.ds(3, 32, stride=4)] + ax_in[step, 1]

    av[...] = -q[0:64]
    last = pltpu.make_async_copy(av, initial_out, store_sem.at[1])
    last.start()
    for copy in ghosts:
        copy.wait_send()
    for step in range(STEPS):

        @pl.when(has_above)
        def _():
            message(step, 1, above).wait_send()

        @pl.when(has_below)
        def _():
            message(step, 0, below).wait_send()

    pltpu.make_async_copy(source, source_out, store_sem.at[0]).wait()
    last.wait()


def per_device(cotangent, off_blocks, diag_inverse):
    vmem, dma = pltpu.VMEM, pltpu.SemaphoreType.DMA
    anywhere = pl.BlockSpec(memory_space=pl.ANY)
    hbm = pl.BlockSpec(memory_space=pltpu.HBM)
    source, initial = pl.pallas_call(
        kernel,
        out_shape=[jax.ShapeDtypeStruct((64, 128), F32)] * 2,
        in_specs=[hbm] * 3,
        out_specs=[anywhere] * 2,
        scratch_shapes=[
            vmem((64, 128), F32),
            vmem((8, 8, 2, 64, 128), BF16),
            vmem((8, 2, 64, 128), BF16),
            vmem((64, 128), F32),
            vmem((8, 64, 128), F32),
            vmem((64, 128), F32),
            vmem((2, 5, 64, 128), BF16),
            vmem((2, 5, 64, 128), BF16),
            vmem((8, 128), F32),
            vmem((2, 8, 128), F32),
            vmem((8, 64, 128), F32),
            vmem((128, 128), F32),
            vmem((128, 128), F32),
            vmem((128, 128), F32),
            vmem((STEPS, 2, 32, 128), F32),
            vmem((STEPS, 2, 32, 128), F32),
            vmem((256, 128), BF16),
            vmem((2, 256, 128), BF16),
            vmem((3, 256, 256), BF16),
            dma((10,)),
            dma((2,)),
            dma((4,)),
            dma((4,)),
            dma((STEPS, 2)),
            dma((STEPS, 2)),
        ],
        compiler_params=pltpu.CompilerParams(
            collective_id=0, has_side_effects=True, vmem_limit_bytes=60 << 20
        ),
        cost_estimate=pl.CostEstimate(
            flops=10 << 20, bytes_accessed=5 << 19, transcendentals=0
        ),
    )(
        cotangent.reshape(64, 128),
        off_blocks.reshape(8, 8, 2, 64, 128),
        diag_inverse.reshape(8, 2, 64, 128),
    )
    return source.reshape(cotangent.shape), initial.reshape(cotangent.shape)


def solution(mesh):
    return jax.shard_map(
        per_device,
        mesh=mesh,
        in_specs=(
            P(None, "ax", "circ"),
            P(None, None, None, "ax", "circ"),
            P(None, None, "ax", "circ"),
        ),
        out_specs=(P(None, "ax", "circ"), P(None, "ax", "circ")),
        check_vma=False,
    )
```

time: 149 us -> 51.7 us (0.35)
  the two profiles are of different devices: /device:TPU:32 before, /device:TPU:14 now
where the time goes in v1:
time: 51.7 us; the launch traced here: 51.4 us
  Pallas kernels  48 us (93%)
  local copies, waits for them, and re-layouts  2.75 us (5%)
  between operations  0.64 us (1%)
    pallas_call x1, Pallas kernels, per_device(): pl.pallas_call(kernel, out_shape=[jax.ShapeDtypeStruct((64, 128), F32)] *...  48 us
    unnamed x2, local copies, waits for them, and re-layouts  2.75 us

profile of v1, /device:TPU:14, one launch (start us, length us, event | category | flops | bytes accessed | tf_op | source)
XLA Modules:
  0.0 51.4 jit_solution(10100512543790325239)
XLA Ops:
  0.6 48.0 %shard_map.50 = (f32[64,128]{1,0:T(8,128)}, f32[64,128]{1,0:T(8,128)}) custom-call(f32[64,128]{1,0:T(8,128)} %bitcast.7, bf16[8,8,2,64,128]{4,3,2,1,0:T(8,128)(2,1)} %bitcast.5, bf16[8,2,64,128]{3,2,1,0:T(8,128)(2,1)} %bitcast.6), custom_call_target="tpu_custom_call" | custom-call | flops 10485760 | bytes 2621440 | tf_op jit(solution)/shard_map/pallas_call | solution.py:349
  48.6 1.4 %copy.7 = f32[16,4,128]{2,1,0:T(4,128)} copy(f32[16,4,128]{2,1,0:T(4,128)} %bitcast.9) | data formatting | bytes 65536
  50.0 1.4 %copy.8 = f32[16,4,128]{2,1,0:T(4,128)} copy(f32[16,4,128]{2,1,0:T(4,128)} %bitcast.8) | data formatting | bytes 65536

commit v2 on v1

v2 whole, which is shorter than its diff:
```python
import functools

import jax
import jax.numpy as jnp
from jax import lax
from jax.experimental import pallas as pl
from jax.experimental.pallas import tpu as pltpu
from jax.sharding import PartitionSpec as P

STEPS = 4
MESH = pl.DeviceIdType.MESH
F32 = jnp.float32
BF16 = jnp.bfloat16


def halves(field):
    sub = lax.broadcasted_iota(jnp.int32, (8, 128), 0)
    out = []
    for v in range(8):
        here = field[8 * v : 8 * v + 8]
        turned = pltpu.roll(here, 4, 0)
        out.append(jnp.where(sub < 4, here, turned))
        out.append(jnp.where(sub < 4, turned, here))
    return out


def spread(field):
    sub = lax.broadcasted_iota(jnp.int32, (8, 128), 0)
    group = lax.broadcasted_iota(jnp.int32, (8, 128), 1) >> 3
    total = jnp.zeros((8, 128), F32)
    for v in range(8):
        total = jnp.where(group == 2 * v + (sub >> 2), field[8 * v : 8 * v + 8], total)
    return total + pltpu.roll(total, 4, 0)


def split(x, parts):
    out = []
    for _ in range(parts):
        part = x.astype(BF16)
        out.append(part)
        x = x - part.astype(F32)
    return out


def times(blocks, rows):
    return (blocks.reshape(8, 8, 128) * rows[None]).reshape(64, 128)


def kernel(
    cot,
    off,
    diag,
    source_out,
    initial_out,
    av,
    bv,
    dv,
    source,
    edge_b,
    ghost_b,
    ghost_a,
    out_b,
    out_a,
    edge_w,
    strip_b,
    strip_d,
    pk,
    up_s,
    down_s,
    q,
    ax_out,
    ax_in,
    pick,
    same,
    moves,
    load_sem,
    store_sem,
    gsend,
    grecv,
    asend,
    arecv,
):
    ax, circ = lax.axis_index("ax"), lax.axis_index("circ")
    n_ax, n_circ = lax.axis_size("ax"), lax.axis_size("circ")
    right = (ax, lax.rem(circ + 1, n_circ))
    left = (ax, lax.rem(circ + n_circ - 1, n_circ))
    above, below = (ax - 1, circ), (ax + 1, circ)
    has_above, has_below = ax > 0, ax < n_ax - 1

    loads = [
        pltpu.make_async_copy(cot, av, load_sem.at[8]),
        pltpu.make_async_copy(diag, dv, load_sem.at[9]),
    ]
    for copy in loads:
        copy.start()

    def load(k):
        return pltpu.make_async_copy(off.at[k], bv.at[k], load_sem.at[k])

    for k in range(8):
        load(k).start()

    barrier = pltpu.get_barrier_semaphore()

    for way, there in ((0, has_above), (1, has_below)):

        @pl.when(jnp.logical_not(there))
        def _(way=way):
            ax_in[:, way] = jnp.zeros((STEPS, 16, 128), F32)
            edge_b[2 * way] = jnp.zeros((9, 64, 128), BF16)
            ghost_b[2 * way] = jnp.zeros((2, 5, 64, 128), BF16)
            ghost_a[2 * way] = jnp.zeros((2, 8, 128), F32)
            edge_w[2 * way] = jnp.zeros((STEPS - 1, 8, 128), F32)

    pl.semaphore_signal(barrier, inc=1, device_id=left, device_id_type=MESH)

    @pl.when(has_above)
    def _():
        pl.semaphore_signal(barrier, inc=1, device_id=above, device_id_type=MESH)

    @pl.when(has_below)
    def _():
        pl.semaphore_signal(barrier, inc=1, device_id=below, device_id_type=MESH)

    row = lax.broadcasted_iota(jnp.int32, (256, 128), 0)
    col = lax.broadcasted_iota(jnp.int32, (256, 128), 1)
    at_edge = ((row + 4) & 127) == (col & 7)
    pick[...] = jnp.where(at_edge & (((col >> 3) & 1) == (row >> 7)), 1.0, 0.0).astype(BF16)
    same[0] = jnp.where((row & 7) == (col & 7), 1.0, 0.0).astype(BF16)
    same[1] = jnp.where(at_edge, 1.0, 0.0).astype(BF16)
    for i, shift in enumerate((-1, 0, 1)):
        moves[i] = jnp.where((col & 7) == (row & 7) + shift, 1.0, 0.0).astype(BF16)

    lane = lax.broadcasted_iota(jnp.int32, (64, 128), 1)
    sub = lax.broadcasted_iota(jnp.int32, (64, 128), 0)
    lane8 = lax.broadcasted_iota(jnp.int32, (8, 128), 1)
    low, low8 = (lane & 7) < 4, (lane8 & 7) < 4

    def pick_edges(blocks):
        both = jnp.concatenate(
            [blocks[:, 0].reshape(512, 128), blocks[:, 1].reshape(512, 128)], axis=1
        )
        found = jnp.dot(both, pick[...], preferred_element_type=F32)
        total = found[0:64]
        for p in range(1, 8):
            total = jnp.where((lane >> 4) == p, found[64 * p : 64 * p + 64], total)
        return total

    def edges_of(field, parts):
        total = jnp.zeros((64, 128), F32)
        for part in split(field, parts):
            total = total + jnp.dot(part, same[1, :128], preferred_element_type=F32)
        return spread(total)

    loads[0].wait()
    field = av[...]
    out_a[...] = edges_of(field, 3)
    loads[1].wait()
    edges = pick_edges(dv[...]).astype(BF16)
    edge_b[1, 8] = edges
    out_b[0, 4] = edges
    out_b[1, 4] = edges
    for half in range(2):
        for k in range(4 * half, 4 * half + 4):
            load(k).wait()
        for pair in (2 * half, 2 * half + 1):
            first = pick_edges(bv[2 * pair])
            second = pick_edges(bv[2 * pair + 1])
            edge_b[1, 2 * pair] = first.astype(BF16)
            edge_b[1, 2 * pair + 1] = second.astype(BF16)
            out_b[0, pair] = jnp.where(low, first, pltpu.roll(second, 4, 1)).astype(BF16)
            out_b[1, pair] = jnp.where(low, pltpu.roll(first, 124, 1), second).astype(BF16)

    pl.semaphore_wait(
        barrier, 1 + has_above.astype(jnp.int32) + has_below.astype(jnp.int32)
    )

    ghosts = []
    for side, target in ((0, right), (1, left)):
        for part, (src, dst) in enumerate(
            ((out_b.at[side], ghost_b.at[1, side]), (out_a, ghost_a.at[1, side]))
        ):
            ghosts.append(
                pltpu.make_async_remote_copy(
                    src_ref=src,
                    dst_ref=dst,
                    send_sem=gsend.at[2 * side + part],
                    recv_sem=grecv.at[2 * side + part],
                    device_id=target,
                    device_id_type=MESH,
                )
            )
    ghosts[0].start()
    ghosts[1].start()

    def along(src, dst, slot, way):
        return pltpu.make_async_remote_copy(
            src_ref=src,
            dst_ref=dst,
            send_sem=asend.at[slot, way],
            recv_sem=arecv.at[slot, way],
            device_id=below if way == 0 else above,
            device_id_type=MESH,
        )

    def rows_copy(step, way):
        return along(ax_out.at[step, way], ax_in.at[step, way], step, way)

    def blocks_copy(way):
        return along(edge_b.at[1], edge_b.at[2 * way], STEPS, way)

    def weighted_copy(way):
        return along(edge_w.at[1], edge_w.at[2 * way], STEPS + 1, way)

    def forward_copies(side, way):
        slot = STEPS + 2 + 2 * side
        return (
            along(ghost_b.at[1, side], ghost_b.at[2 * way, side], slot, way),
            along(ghost_a.at[1, side], ghost_a.at[2 * way, side], slot + 1, way),
        )

    def start(copies):
        for way, there in ((0, has_below), (1, has_above)):

            @pl.when(there)
            def _(way=way):
                for copy in copies(way):
                    copy.start()

    def arrive(copies):
        for way, there in ((0, has_above), (1, has_below)):

            @pl.when(there)
            def _(way=way):
                for copy in copies(way):
                    copy.wait_recv()

    def sent(copies):
        for way, there in ((0, has_below), (1, has_above)):

            @pl.when(there)
            def _(way=way):
                for copy in copies(way):
                    copy.wait_send()

    for step in range(STEPS):
        rows = halves(field)
        w = jnp.zeros((64, 128), F32)
        for r in range(16):
            w = w + times(dv[r // 2, r % 2].astype(F32), rows[r])
        source[...] = w if step == 0 else source[...] + w
        rows = halves(w)

        @pl.loop(0, 8)
        def _(k):
            total = jnp.zeros((64, 128), F32)
            for r in range(16):
                total = total + times(bv[k, r // 2, r % 2].astype(F32), rows[r])
            pk[k] = total

        def gathered(slot_left, slot_same, slot_right):
            main = jnp.where(lane == 127, 0.0, pltpu.roll(pk[slot_left], 127, 1))
            main = main + jnp.where(lane == 0, 0.0, pltpu.roll(pk[slot_right], 1, 1))
            return main if slot_same is None else main + pk[slot_same]

        up = gathered(0, 1, 2)
        down = gathered(5, 6, 7)
        up_s[...] = up
        down_s[...] = down
        ax_out[step, 1] = up_s[pl.ds(0, 16, stride=4)]
        ax_out[step, 0] = down_s[pl.ds(3, 16, stride=4)]
        start(lambda way, step=step: [rows_copy(step, way)])
        if step == 0:
            start(lambda way: [blocks_copy(way)])
        if step < STEPS - 1:
            edge_w[1, step] = edges_of(w, 2)
        if step == STEPS - 2:
            start(lambda way: [weighted_copy(way)])
        lifted = pltpu.roll(up.reshape(8, 8, 128), 7, 1).reshape(64, 128)
        dropped = pltpu.roll(down.reshape(8, 8, 128), 1, 1).reshape(64, 128)
        q[...] = (
            gathered(3, None, 4)
            + jnp.where((sub & 3) == 3, 0.0, lifted)
            + jnp.where((sub & 3) == 0, 0.0, dropped)
        )
        if step >= STEPS - 2:
            side = step - (STEPS - 2)
            ghosts[2 * side].wait_recv()
            ghosts[2 * side + 1].wait_recv()
            if side == 0:
                ghosts[2].start()
                ghosts[3].start()
            start(lambda way, side=side: forward_copies(side, way))
        arrive(lambda way, step=step: [rows_copy(step, way)])
        q[pl.ds(0, 16, stride=4)] = q[pl.ds(0, 16, stride=4)] + ax_in[step, 0]
        q[pl.ds(3, 16, stride=4)] = q[pl.ds(3, 16, stride=4)] + ax_in[step, 1]
        field = -q[...]
    av[...] = field

    def assemble(side, block):
        for pair in range(4):
            ghost = ghost_b[block, side, pair].astype(F32)
            first = edge_b[block, 2 * pair].astype(F32)
            second = edge_b[block, 2 * pair + 1].astype(F32)
            if side == 0:
                strip_b[side, block, 2 * pair] = jnp.where(low, ghost, first)
                strip_b[side, block, 2 * pair + 1] = jnp.where(
                    low, pltpu.roll(ghost, 124, 1), second
                )
            else:
                strip_b[side, block, 2 * pair] = jnp.where(low, first, pltpu.roll(ghost, 4, 1))
                strip_b[side, block, 2 * pair + 1] = jnp.where(low, second, ghost)
        ghost = ghost_b[block, side, 4].astype(F32)
        mine = edge_b[block, 8].astype(F32)
        strip_d[side, block] = (
            jnp.where(low, ghost, mine) if side == 0 else jnp.where(low, mine, ghost)
        )

    def strip(side):
        arrive(lambda way: forward_copies(side, way))
        for block in range(3):
            assemble(side, block)
        blocks = range(3)
        outward = (0, 3, 5) if side == 0 else (2, 4, 7)
        crossing = (lane8 & 7) == (4 if side == 0 else 3)
        d, added = None, None
        for step in range(STEPS):
            if step == 0:
                fields = [ghost_a[block, side] for block in blocks]
                if side == 0:
                    fields = [jnp.where(low8, a, 0.0) for a in fields]
                else:
                    fields = [jnp.where(low8, 0.0, a) for a in fields]
            else:
                fields = [spread(x) for x in d]
            p = [times(strip_d[side, block], fields[block]) for block in blocks]
            w = jnp.dot(
                jnp.concatenate(split(jnp.concatenate(p, axis=0), 2), axis=1),
                same[0],
                preferred_element_type=F32,
            )
            added = w[64:128] if step == 0 else added + w[64:128]
            rows = [spread(w[64 * block : 64 * block + 64]) for block in blocks]
            rows_out = rows
            if step < STEPS - 1:
                rows_out = [
                    rows[block] + jnp.where(crossing, edge_w[block, step], 0.0)
                    for block in blocks
                ]

            def flow(k, block):
                return times(
                    strip_b[side, block, k], (rows_out if k in outward else rows)[block]
                )

            def turned(x, by):
                return pltpu.roll(x.reshape(8, 8, 128), by, 1).reshape(64, 128)

            targets = blocks if step < STEPS - 1 else (1,)
            moved = jnp.zeros((64 * len(targets), 128), F32)
            for i, (k_up, k_level, k_down) in enumerate(((0, 3, 5), (1, None, 6), (2, 4, 7))):
                ups = {block: flow(k_up, block) for block in blocks}
                downs = {block: flow(k_down, block) for block in blocks}
                sums = []
                for block in targets:
                    total = turned(ups[block], 7)
                    over = turned(ups[block + 1], 3) if block < 2 else 0.0
                    total = jnp.where((sub & 3) == 3, over, total)
                    falling = turned(downs[block], 1)
                    over = turned(downs[block - 1], 5) if block > 0 else 0.0
                    total = total + jnp.where((sub & 3) == 0, over, falling)
                    if k_level is not None:
                        total = total + flow(k_level, block)
                    sums.append(total)
                moved = moved + jnp.dot(
                    jnp.concatenate(split(jnp.concatenate(sums, axis=0), 2), axis=1),
                    moves[i],
                    preferred_element_type=F32,
                )
            d = [-moved[64 * n : 64 * n + 64] for n in range(len(targets))]
        return added, d[0]

    arrive(lambda way: [blocks_copy(way)])
    arrive(lambda way: [weighted_copy(way)])
    added_right, d_right = strip(1)
    added_left, d_left = strip(0)

    def with_strips(u, left_strip, right_strip):
        u = u + jnp.where(lane < 4, pltpu.roll(left_strip, 124, 1), 0.0)
        return u + jnp.where(lane >= 124, pltpu.roll(right_strip, 4, 1), 0.0)

    source[...] = with_strips(source[...], added_left, added_right)
    av[...] = with_strips(av[...], d_left, d_right)
    stores = [
        pltpu.make_async_copy(source, source_out, store_sem.at[0]),
        pltpu.make_async_copy(av, initial_out, store_sem.at[1]),
    ]
    for copy in stores:
        copy.start()
    for copy in ghosts:
        copy.wait_send()
    for step in range(STEPS):
        sent(lambda way, step=step: [rows_copy(step, way)])
    sent(lambda way: [blocks_copy(way), weighted_copy(way)])
    for side in range(2):
        sent(lambda way, side=side: forward_copies(side, way))
    for copy in stores:
        copy.wait()


def per_device(cotangent, off_blocks, diag_inverse):
    vmem, dma = pltpu.VMEM, pltpu.SemaphoreType.DMA
    anywhere = pl.BlockSpec(memory_space=pl.ANY)
    hbm = pl.BlockSpec(memory_space=pltpu.HBM)
    source, initial = pl.pallas_call(
        kernel,
        out_shape=[jax.ShapeDtypeStruct((64, 128), F32)] * 2,
        in_specs=[hbm] * 3,
        out_specs=[anywhere] * 2,
        scratch_shapes=[
            vmem((64, 128), F32),
            vmem((8, 8, 2, 64, 128), BF16),
            vmem((8, 2, 64, 128), BF16),
            vmem((64, 128), F32),
            vmem((3, 9, 64, 128), BF16),
            vmem((3, 2, 5, 64, 128), BF16),
            vmem((3, 2, 8, 128), F32),
            vmem((2, 5, 64, 128), BF16),
            vmem((8, 128), F32),
            vmem((3, STEPS - 1, 8, 128), F32),
            vmem((2, 3, 8, 64, 128), F32),
            vmem((2, 3, 64, 128), F32),
            vmem((8, 64, 128), F32),
            vmem((64, 128), F32),
            vmem((64, 128), F32),
            vmem((64, 128), F32),
            vmem((STEPS, 2, 16, 128), F32),
            vmem((STEPS, 2, 16, 128), F32),
            vmem((256, 128), BF16),
            vmem((2, 256, 128), BF16),
            vmem((3, 256, 128), BF16),
            dma((10,)),
            dma((2,)),
            dma((4,)),
            dma((4,)),
            dma((STEPS + 6, 2)),
            dma((STEPS + 6, 2)),
        ],
        compiler_params=pltpu.CompilerParams(
            collective_id=0, has_side_effects=True, vmem_limit_bytes=60 << 20
        ),
        cost_estimate=pl.CostEstimate(
            flops=10 << 20, bytes_accessed=5 << 19, transcendentals=0
        ),
    )(
        cotangent.reshape(64, 128),
        off_blocks.reshape(8, 8, 2, 64, 128),
        diag_inverse.reshape(8, 2, 64, 128),
    )
    return source.reshape(cotangent.shape), initial.reshape(cotangent.shape)


def solution(mesh):
    return jax.shard_map(
        per_device,
        mesh=mesh,
        in_specs=(
            P(None, "ax", "circ"),
            P(None, None, None, "ax", "circ"),
            P(None, None, "ax", "circ"),
        ),
        out_specs=(P(None, "ax", "circ"), P(None, "ax", "circ")),
        check_vma=False,
    )
```

time: 51.7 us -> 43.8 us (0.85)
  the two profiles are of different devices: /device:TPU:14 before, /device:TPU:32 now
where the time goes in v2:
time: 43.8 us; the launch traced here: 43.5 us
  Pallas kernels  40.1 us (92%)
  local copies, waits for them, and re-layouts  2.75 us (6%)
  between operations  0.64 us (1%)
    pallas_call x1, Pallas kernels, per_device(): pl.pallas_call(kernel, out_shape=[jax.ShapeDtypeStruct((64, 128), F32)] *...  40.1 us
    unnamed x2, local copies, waits for them, and re-layouts  2.75 us

profile of v2, /device:TPU:32, one launch (start us, length us, event | category | flops | bytes accessed | tf_op | source)
XLA Modules:
  0.0 43.5 jit_solution(9367376237395414921)
XLA Ops:
  0.6 40.1 %shard_map.50 = (f32[64,128]{1,0:T(8,128)}, f32[64,128]{1,0:T(8,128)}) custom-call(f32[64,128]{1,0:T(8,128)} %bitcast.7, bf16[8,8,2,64,128]{4,3,2,1,0:T(8,128)(2,1)} %bitcast.5, bf16[8,2,64,128]{3,2,1,0:T(8,128)(2,1)} %bitcast.6), custom_call_target="tpu_custom_call" | custom-call | flops 10485760 | bytes 2621440 | tf_op jit(solution)/shard_map/pallas_call | solution.py:415
  40.7 1.4 %copy.7 = f32[16,4,128]{2,1,0:T(4,128)} copy(f32[16,4,128]{2,1,0:T(4,128)} %bitcast.9) | data formatting | bytes 65536
  42.1 1.4 %copy.8 = f32[16,4,128]{2,1,0:T(4,128)} copy(f32[16,4,128]{2,1,0:T(4,128)} %bitcast.8) | data formatting | bytes 65536

commit v3 on v2

--- a/solution.py
+++ b/solution.py
@@ -11,6 +11,8 @@
 MESH = pl.DeviceIdType.MESH
 F32 = jnp.float32
 BF16 = jnp.bfloat16
+
+SLOTS = (((2, 4, 7), (1, 6), (0, 3, 5)), ((0, 3, 5), (1, 6), (2, 4, 7)))
 
 
 def halves(field):
@@ -70,7 +72,7 @@
     q,
     ax_out,
     ax_in,
-    pick,
+    pick_s,
     same,
     moves,
     load_sem,
@@ -97,8 +99,9 @@
     def load(k):
         return pltpu.make_async_copy(off.at[k], bv.at[k], load_sem.at[k])
 
-    for k in range(8):
-        load(k).start()
+    for group in SLOTS[0]:
+        for k in group:
+            load(k).start()
 
     barrier = pltpu.get_barrier_semaphore()
 
@@ -108,7 +111,7 @@
         def _(way=way):
             ax_in[:, way] = jnp.zeros((STEPS, 16, 128), F32)
             edge_b[2 * way] = jnp.zeros((9, 64, 128), BF16)
-            ghost_b[2 * way] = jnp.zeros((2, 5, 64, 128), BF16)
+            ghost_b[2 * way] = jnp.zeros((2, 4, 64, 128), BF16)
             ghost_a[2 * way] = jnp.zeros((2, 8, 128), F32)
             edge_w[2 * way] = jnp.zeros((STEPS - 1, 8, 128), F32)
 
@@ -125,7 +128,7 @@
     row = lax.broadcasted_iota(jnp.int32, (256, 128), 0)
     col = lax.broadcasted_iota(jnp.int32, (256, 128), 1)
     at_edge = ((row + 4) & 127) == (col & 7)
-    pick[...] = jnp.where(at_edge & (((col >> 3) & 1) == (row >> 7)), 1.0, 0.0).astype(BF16)
+    pick_s[...] = jnp.where(at_edge & (((col >> 3) & 1) == (row >> 7)), 1.0, 0.0).astype(BF16)
     same[0] = jnp.where((row & 7) == (col & 7), 1.0, 0.0).astype(BF16)
     same[1] = jnp.where(at_edge, 1.0, 0.0).astype(BF16)
     for i, shift in enumerate((-1, 0, 1)):
@@ -140,7 +143,7 @@
         both = jnp.concatenate(
             [blocks[:, 0].reshape(512, 128), blocks[:, 1].reshape(512, 128)], axis=1
         )
-        found = jnp.dot(both, pick[...], preferred_element_type=F32)
+        found = jnp.dot(both, pick_s[...], preferred_element_type=F32)
         total = found[0:64]
         for p in range(1, 8):
             total = jnp.where((lane >> 4) == p, found[64 * p : 64 * p + 64], total)
@@ -156,21 +159,33 @@
     field = av[...]
     out_a[...] = edges_of(field, 3)
     loads[1].wait()
-    edges = pick_edges(dv[...]).astype(BF16)
-    edge_b[1, 8] = edges
-    out_b[0, 4] = edges
-    out_b[1, 4] = edges
-    for half in range(2):
-        for k in range(4 * half, 4 * half + 4):
+    picked = {8: pick_edges(dv[...])}
+
+    def pick(slots):
+        for k in slots:
             load(k).wait()
-        for pair in (2 * half, 2 * half + 1):
-            first = pick_edges(bv[2 * pair])
-            second = pick_edges(bv[2 * pair + 1])
-            edge_b[1, 2 * pair] = first.astype(BF16)
-            edge_b[1, 2 * pair + 1] = second.astype(BF16)
-            out_b[0, pair] = jnp.where(low, first, pltpu.roll(second, 4, 1)).astype(BF16)
-            out_b[1, pair] = jnp.where(low, pltpu.roll(first, 124, 1), second).astype(BF16)
-
+        for k in slots:
+            picked[k] = pick_edges(bv[k])
+
+    def pair(first, second):
+        return jnp.where(low, picked[first], pltpu.roll(picked[second], 4, 1))
+
+    def pair_high(first, second):
+        return jnp.where(low, pltpu.roll(picked[first], 124, 1), picked[second])
+
+    ghost = lane & 7
+
+    def three(slots, at):
+        total = jnp.where(ghost < 2, pltpu.roll(picked[slots[0]], (128 - at) % 128, 1), 0.0)
+        for n in (1, 2):
+            moved = pltpu.roll(picked[slots[n]], (128 + 2 * n - at) % 128, 1)
+            total = jnp.where((ghost >> 1) == n, moved, total)
+        return total
+
+    towards, level, away = SLOTS[0]
+    pick(towards)
+    out_b[0, 0] = pair(towards[0], towards[1]).astype(BF16)
+    out_b[0, 1] = pair(towards[2], 8).astype(BF16)
     pl.semaphore_wait(
         barrier, 1 + has_above.astype(jnp.int32) + has_below.astype(jnp.int32)
     )
@@ -178,20 +193,35 @@
     ghosts = []
     for side, target in ((0, right), (1, left)):
         for part, (src, dst) in enumerate(
-            ((out_b.at[side], ghost_b.at[1, side]), (out_a, ghost_a.at[1, side]))
+            (
+                (out_a, ghost_a.at[1, side]),
+                (out_b.at[side, 0:2], ghost_b.at[1, side, 0:2]),
+                (out_b.at[side, 2:4], ghost_b.at[1, side, 2:4]),
+            )
         ):
             ghosts.append(
                 pltpu.make_async_remote_copy(
                     src_ref=src,
                     dst_ref=dst,
-                    send_sem=gsend.at[2 * side + part],
-                    recv_sem=grecv.at[2 * side + part],
+                    send_sem=gsend.at[side, part],
+                    recv_sem=grecv.at[side, part],
                     device_id=target,
                     device_id_type=MESH,
                 )
             )
+    ghosts[1].start()
     ghosts[0].start()
-    ghosts[1].start()
+    pick(level + away)
+    out_b[0, 2] = pair(*level).astype(BF16)
+    out_b[0, 3] = three(away, 2).astype(BF16)
+    ghosts[2].start()
+    for k in range(9):
+        edge_b[1, k] = picked[k].astype(BF16)
+    towards, level, away = SLOTS[1]
+    out_b[1, 0] = pair_high(towards[0], towards[1]).astype(BF16)
+    out_b[1, 1] = pair_high(towards[2], 8).astype(BF16)
+    out_b[1, 2] = pair_high(*level).astype(BF16)
+    out_b[1, 3] = three(away, 4).astype(BF16)
 
     def along(src, dst, slot, way):
         return pltpu.make_async_remote_copy(
@@ -212,12 +242,18 @@
     def weighted_copy(way):
         return along(edge_w.at[1], edge_w.at[2 * way], STEPS + 1, way)
 
+    def forward_copy(side, part, way):
+        ref = (ghost_a, ghost_b, ghost_b)[part]
+        at = ((), (slice(0, 2),), (slice(2, 4),))[part]
+        return along(
+            ref.at[(1, side) + at],
+            ref.at[(2 * way, side) + at],
+            STEPS + 2 + 3 * side + part,
+            way,
+        )
+
     def forward_copies(side, way):
-        slot = STEPS + 2 + 2 * side
-        return (
-            along(ghost_b.at[1, side], ghost_b.at[2 * way, side], slot, way),
-            along(ghost_a.at[1, side], ghost_a.at[2 * way, side], slot + 1, way),
-        )
+        return [forward_copy(side, part, way) for part in range(3)]
 
     def start(copies):
         for way, there in ((0, has_below), (1, has_above)):
@@ -242,6 +278,16 @@
             def _(way=way):
                 for copy in copies(way):
                     copy.wait_send()
+
+    def pass_on(side):
+        for part in (1, 0, 2):
+            ghosts[3 * side + part].wait_recv()
+            if part != 1:
+                parts = (0, 1) if part == 0 else (2,)
+                start(lambda way: [forward_copy(side, n, way) for n in parts])
+        if side == 0:
+            for copy in ghosts[3:]:
+                copy.start()
 
     for step in range(STEPS):
         rows = halves(field)
@@ -283,14 +329,19 @@
             + jnp.where((sub & 3) == 3, 0.0, lifted)
             + jnp.where((sub & 3) == 0, 0.0, dropped)
         )
-        if step >= STEPS - 2:
-            side = step - (STEPS - 2)
-            ghosts[2 * side].wait_recv()
-            ghosts[2 * side + 1].wait_recv()
-            if side == 0:
-                ghosts[2].start()
-                ghosts[3].start()
-            start(lambda way, side=side: forward_copies(side, way))
+        if step == STEPS - 2:
+
+            @pl.when(circ > 0)
+            def _():
+                pass_on(0)
+
+        if step == STEPS - 1:
+            pass_on(1)
+
+            @pl.when(circ == 0)
+            def _():
+                pass_on(0)
+
         arrive(lambda way, step=step: [rows_copy(step, way)])
         q[pl.ds(0, 16, stride=4)] = q[pl.ds(0, 16, stride=4)] + ax_in[step, 0]
         q[pl.ds(3, 16, stride=4)] = q[pl.ds(3, 16, stride=4)] + ax_in[step, 1]
@@ -298,28 +349,28 @@
     av[...] = field
 
     def assemble(side, block):
-        for pair in range(4):
-            ghost = ghost_b[block, side, pair].astype(F32)
-            first = edge_b[block, 2 * pair].astype(F32)
-            second = edge_b[block, 2 * pair + 1].astype(F32)
-            if side == 0:
-                strip_b[side, block, 2 * pair] = jnp.where(low, ghost, first)
-                strip_b[side, block, 2 * pair + 1] = jnp.where(
-                    low, pltpu.roll(ghost, 124, 1), second
-                )
-            else:
-                strip_b[side, block, 2 * pair] = jnp.where(low, first, pltpu.roll(ghost, 4, 1))
-                strip_b[side, block, 2 * pair + 1] = jnp.where(low, second, ghost)
-        ghost = ghost_b[block, side, 4].astype(F32)
-        mine = edge_b[block, 8].astype(F32)
-        strip_d[side, block] = (
-            jnp.where(low, ghost, mine) if side == 0 else jnp.where(low, mine, ghost)
-        )
+        towards, level, away = SLOTS[side]
+        parts = [ghost_b[block, side, n].astype(F32) for n in range(4)]
+
+        def put(to, k, part, by):
+            found = pltpu.roll(parts[part], by % 128, 1) if by else parts[part]
+            mine = edge_b[block, k].astype(F32)
+            to[...] = jnp.where(low if side == 0 else ~low, found, mine)
+
+        base = 4 * side
+        for n, k in enumerate(towards):
+            put(strip_b.at[side, block, k], k, n // 2, base - 4 * (n % 2))
+        put(strip_d.at[side, block], 8, 1, base - 4)
+        for n, k in enumerate(level):
+            put(strip_b.at[side, block, k], k, 2, base - 4 * n)
+        for n, k in enumerate(away):
+            put(strip_b.at[side, block, k], k, 3, (2 if side == 0 else 4) - 2 * n)
 
     def strip(side):
+        assemble(side, 1)
         arrive(lambda way: forward_copies(side, way))
-        for block in range(3):
-            assemble(side, block)
+        assemble(side, 0)
+        assemble(side, 2)
         blocks = range(3)
         outward = (0, 3, 5) if side == 0 else (2, 4, 7)
         crossing = (lane8 & 7) == (4 if side == 0 else 3)
@@ -408,6 +459,11 @@
         copy.wait()
 
 
+def written(source, initial, source_out, initial_out):
+    source_out[...] = source[...]
+    initial_out[...] = initial[...]
+
+
 def per_device(cotangent, off_blocks, diag_inverse):
     vmem, dma = pltpu.VMEM, pltpu.SemaphoreType.DMA
     anywhere = pl.BlockSpec(memory_space=pl.ANY)
@@ -423,9 +479,9 @@
             vmem((8, 2, 64, 128), BF16),
             vmem((64, 128), F32),
             vmem((3, 9, 64, 128), BF16),
-            vmem((3, 2, 5, 64, 128), BF16),
+            vmem((3, 2, 4, 64, 128), BF16),
             vmem((3, 2, 8, 128), F32),
-            vmem((2, 5, 64, 128), BF16),
+            vmem((2, 4, 64, 128), BF16),
             vmem((8, 128), F32),
             vmem((3, STEPS - 1, 8, 128), F32),
             vmem((2, 3, 8, 64, 128), F32),
@@ -441,10 +497,10 @@
             vmem((3, 256, 128), BF16),
             dma((10,)),
             dma((2,)),
-            dma((4,)),
-            dma((4,)),
-            dma((STEPS + 6, 2)),
-            dma((STEPS + 6, 2)),
+            dma((2, 3)),
+            dma((2, 3)),
+            dma((STEPS + 8, 2)),
+            dma((STEPS + 8, 2)),
         ],
         compiler_params=pltpu.CompilerParams(
             collective_id=0, has_side_effects=True, vmem_limit_bytes=60 << 20
@@ -457,6 +513,12 @@
         off_blocks.reshape(8, 8, 2, 64, 128),
         diag_inverse.reshape(8, 2, 64, 128),
     )
+    source, initial = pl.pallas_call(
+        written,
+        out_shape=[jax.ShapeDtypeStruct((64, 128), F32)] * 2,
+        in_specs=[pl.BlockSpec(memory_space=vmem)] * 2,
+        out_specs=[pl.BlockSpec(memory_space=vmem)] * 2,
+    )(source, initial)
     return source.reshape(cotangent.shape), initial.reshape(cotangent.shape)
 
 

time: 43.8 us -> 36.5 us (0.83)
  Pallas kernels: 40.1 us -> 35.6 us
  local copies, waits for them, and re-layouts: 2.75 us -> 0 us
    pallas_call x1, Pallas kernels: 40.1 us -> 34.2 us  [per_device(): pl.pallas_call(kernel, out_shape=[jax.ShapeDtypeStruct((64, 128), F32)] *...]
    unnamed x2 -> x0, local copies, waits for them, and re-layouts: 2.75 us -> none
    pallas_call x0 -> x1, Pallas kernels: none -> 1.4 us  [per_device(): pl.pallas_call(written, out_shape=[jax.ShapeDtypeStruct((64, 128), F32)]...]
where the time goes in v3:
time: 36.5 us; the launch traced here: 36.3 us
  Pallas kernels  35.6 us (98%)
  between operations  0.64 us (2%)
    pallas_call x1, Pallas kernels, per_device(): pl.pallas_call(kernel, out_shape=[jax.ShapeDtypeStruct((64, 128), F32)] *...  34.2 us
    pallas_call x1, Pallas kernels, per_device(): pl.pallas_call(written, out_shape=[jax.ShapeDtypeStruct((64, 128), F32)]...  1.4 us

profile of v3, /device:TPU:32, one launch (start us, length us, event | category | flops | bytes accessed | tf_op | source)
XLA Modules:
  0.0 36.3 jit_solution(11972460018746664664)
XLA Ops:
  0.6 34.2 %shard_map.50 = (f32[64,128]{1,0:T(8,128)}, f32[64,128]{1,0:T(8,128)}) custom-call(f32[64,128]{1,0:T(8,128)} %bitcast.7, bf16[8,8,2,64,128]{4,3,2,1,0:T(8,128)(2,1)} %bitcast.5, bf16[8,2,64,128]{3,2,1,0:T(8,128)(2,1)} %bitcast.6), custom_call_target="tpu_custom_call" | custom-call | flops 10485760 | bytes 2621440 | tf_op jit(solution)/shard_map/pallas_call | solution.py:471
  34.9 1.4 %shard_map.51 = (f32[64,128]{1,0:T(8,128)}, f32[64,128]{1,0:T(8,128)}) custom-call(f32[64,128]{1,0:T(8,128)} %get-tuple-element.6.source, f32[64,128]{1,0:T(8,128)} %get-tuple-element.7.initial), custom_call_target="tpu_custom_call" | custom-call | tf_op jit(solution)/shard_map/pallas_call | solution.py:516

commit v4 on v3

--- a/solution.py
+++ b/solution.py
@@ -76,7 +76,6 @@
     same,
     moves,
     load_sem,
-    store_sem,
     gsend,
     grecv,
     asend,
@@ -346,7 +345,6 @@
         q[pl.ds(0, 16, stride=4)] = q[pl.ds(0, 16, stride=4)] + ax_in[step, 0]
         q[pl.ds(3, 16, stride=4)] = q[pl.ds(3, 16, stride=4)] + ax_in[step, 1]
         field = -q[...]
-    av[...] = field
 
     def assemble(side, block):
         towards, level, away = SLOTS[side]
@@ -440,14 +438,8 @@
         u = u + jnp.where(lane < 4, pltpu.roll(left_strip, 124, 1), 0.0)
         return u + jnp.where(lane >= 124, pltpu.roll(right_strip, 4, 1), 0.0)
 
-    source[...] = with_strips(source[...], added_left, added_right)
-    av[...] = with_strips(av[...], d_left, d_right)
-    stores = [
-        pltpu.make_async_copy(source, source_out, store_sem.at[0]),
-        pltpu.make_async_copy(av, initial_out, store_sem.at[1]),
-    ]
-    for copy in stores:
-        copy.start()
+    source_out[...] = with_strips(source[...], added_left, added_right)
+    initial_out[...] = with_strips(field, d_left, d_right)
     for copy in ghosts:
         copy.wait_send()
     for step in range(STEPS):
@@ -455,8 +447,6 @@
     sent(lambda way: [blocks_copy(way), weighted_copy(way)])
     for side in range(2):
         sent(lambda way, side=side: forward_copies(side, way))
-    for copy in stores:
-        copy.wait()
 
 
 def written(source, initial, source_out, initial_out):
@@ -470,9 +460,9 @@
     hbm = pl.BlockSpec(memory_space=pltpu.HBM)
     source, initial = pl.pallas_call(
         kernel,
-        out_shape=[jax.ShapeDtypeStruct((64, 128), F32)] * 2,
+        out_shape=[pltpu.VMEM((64, 128), F32)] * 2,
         in_specs=[hbm] * 3,
-        out_specs=[anywhere] * 2,
+        out_specs=[pl.BlockSpec(memory_space=vmem)] * 2,
         scratch_shapes=[
             vmem((64, 128), F32),
             vmem((8, 8, 2, 64, 128), BF16),
@@ -496,7 +486,6 @@
             vmem((2, 256, 128), BF16),
             vmem((3, 256, 128), BF16),
             dma((10,)),
-            dma((2,)),
             dma((2, 3)),
             dma((2, 3)),
             dma((STEPS + 8, 2)),
@@ -518,7 +507,10 @@
         out_shape=[jax.ShapeDtypeStruct((64, 128), F32)] * 2,
         in_specs=[pl.BlockSpec(memory_space=vmem)] * 2,
         out_specs=[pl.BlockSpec(memory_space=vmem)] * 2,
-    )(source, initial)
+    )(
+        pltpu.with_memory_space_constraint(source, vmem),
+        pltpu.with_memory_space_constraint(initial, vmem),
+    )
     return source.reshape(cotangent.shape), initial.reshape(cotangent.shape)
 
 

time: 36.5 us -> 35.1 us (0.962)
  Pallas kernels: 35.6 us -> 34.3 us
    pallas_call x1, Pallas kernels: 1.4 us -> 0.63 us  [per_device(): pl.pallas_call(written, out_shape=[jax.ShapeDtypeStruct((64, 128), F32)]...]
    pallas_call x1, Pallas kernels: 34.2 us -> 33.7 us  [per_device(): pl.pallas_call(kernel, out_shape=[pltpu.VMEM((64, 128), F32)] * 2, in_spe...]
where the time goes in v4:
time: 35.1 us; the launch traced here: 34.9 us
  Pallas kernels  34.3 us (98%)
  between operations  0.64 us (2%)
    pallas_call x1, Pallas kernels, per_device(): pl.pallas_call(kernel, out_shape=[pltpu.VMEM((64, 128), F32)] * 2, in_spe...  33.7 us

profile of v4, /device:TPU:32, one launch (start us, length us, event | category | flops | bytes accessed | tf_op | source)
XLA Modules:
  0.0 34.9 jit_solution(8560097875087444038)
XLA Ops:
  0.6 33.7 %shard_map.50 = (f32[64,128]{1,0:T(8,128)S(1)}, f32[64,128]{1,0:T(8,128)S(1)}) custom-call(f32[64,128]{1,0:T(8,128)} %bitcast.7, bf16[8,8,2,64,128]{4,3,2,1,0:T(8,128)(2,1)} %bitcast.5, bf16[8,2,64,128]{3,2,1,0:T(8,128)(2,1)} %bitcast.6), custom_call_target="tpu_custom_call" | custom-call | flops 10485760 | bytes 2621440 | tf_op jit(solution)/shard_map/pallas_call | solution.py:461
  34.3 0.6 %shard_map.51 = (f32[64,128]{1,0:T(8,128)}, f32[64,128]{1,0:T(8,128)}) custom-call(f32[64,128]{1,0:T(8,128)S(1)} %get-tuple-element.6.source, f32[64,128]{1,0:T(8,128)S(1)} %get-tuple-element.7.initial), custom_call_target="tpu_custom_call" | custom-call | tf_op jit(solution)/shard_map/pallas_call | solution.py:505

commit v5 on v4

--- a/solution.py
+++ b/solution.py
@@ -208,12 +208,21 @@
                     device_id_type=MESH,
                 )
             )
-    ghosts[1].start()
-    ghosts[0].start()
+    gives_way = circ == n_circ - 3
+
+    @pl.when(jnp.logical_not(gives_way))
+    def _():
+        ghosts[1].start()
+        ghosts[0].start()
+
     pick(level + away)
     out_b[0, 2] = pair(*level).astype(BF16)
     out_b[0, 3] = three(away, 2).astype(BF16)
-    ghosts[2].start()
+
+    @pl.when(jnp.logical_not(gives_way))
+    def _():
+        ghosts[2].start()
+
     for k in range(9):
         edge_b[1, k] = picked[k].astype(BF16)
     towards, level, away = SLOTS[1]
@@ -342,6 +351,13 @@
                 pass_on(0)
 
         arrive(lambda way, step=step: [rows_copy(step, way)])
+        if step == 0:
+
+            @pl.when(gives_way)
+            def _():
+                for part in (1, 0, 2):
+                    ghosts[part].start()
+
         q[pl.ds(0, 16, stride=4)] = q[pl.ds(0, 16, stride=4)] + ax_in[step, 0]
         q[pl.ds(3, 16, stride=4)] = q[pl.ds(3, 16, stride=4)] + ax_in[step, 1]
         field = -q[...]
@@ -406,8 +422,8 @@
                 return pltpu.roll(x.reshape(8, 8, 128), by, 1).reshape(64, 128)
 
             targets = blocks if step < STEPS - 1 else (1,)
-            moved = jnp.zeros((64 * len(targets), 128), F32)
-            for i, (k_up, k_level, k_down) in enumerate(((0, 3, 5), (1, None, 6), (2, 4, 7))):
+            moved = []
+            for k_up, k_level, k_down in ((0, 3, 5), (1, None, 6), (2, 4, 7)):
                 ups = {block: flow(k_up, block) for block in blocks}
                 downs = {block: flow(k_down, block) for block in blocks}
                 sums = []
@@ -421,17 +437,25 @@
                     if k_level is not None:
                         total = total + flow(k_level, block)
                     sums.append(total)
-                moved = moved + jnp.dot(
-                    jnp.concatenate(split(jnp.concatenate(sums, axis=0), 2), axis=1),
-                    moves[i],
-                    preferred_element_type=F32,
-                )
+                moved += split(jnp.concatenate(sums, axis=0), 2)
+            moved = jnp.dot(
+                jnp.concatenate(moved, axis=1),
+                moves[...].reshape(768, 128),
+                preferred_element_type=F32,
+            )
             d = [-moved[64 * n : 64 * n + 64] for n in range(len(targets))]
         return added, d[0]
 
     arrive(lambda way: [blocks_copy(way)])
     arrive(lambda way: [weighted_copy(way)])
     added_right, d_right = strip(1)
+    for copy in ghosts[:3]:
+        copy.wait_send()
+    sent(
+        lambda way: [rows_copy(step, way) for step in range(STEPS)]
+        + [blocks_copy(way), weighted_copy(way)]
+        + forward_copies(1, way)
+    )
     added_left, d_left = strip(0)
 
     def with_strips(u, left_strip, right_strip):
@@ -440,13 +464,9 @@
 
     source_out[...] = with_strips(source[...], added_left, added_right)
     initial_out[...] = with_strips(field, d_left, d_right)
-    for copy in ghosts:
+    for copy in ghosts[3:]:
         copy.wait_send()
-    for step in range(STEPS):
-        sent(lambda way, step=step: [rows_copy(step, way)])
-    sent(lambda way: [blocks_copy(way), weighted_copy(way)])
-    for side in range(2):
-        sent(lambda way, side=side: forward_copies(side, way))
+    sent(lambda way: forward_copies(0, way))
 
 
 def written(source, initial, source_out, initial_out):

time: 35.1 us -> 34.7 us (0.989)
  Pallas kernels: 34.3 us -> 33.9 us
    pallas_call x1, Pallas kernels: 33.7 us -> 33.2 us  [per_device(): pl.pallas_call(kernel, out_shape=[pltpu.VMEM((64, 128), F32)] * 2, in_spe...]
where the time goes in v5:
time: 34.7 us; the launch traced here: 34.5 us
  Pallas kernels  33.9 us (98%)
  between operations  0.64 us (2%)
    pallas_call x1, Pallas kernels, per_device(): pl.pallas_call(kernel, out_shape=[pltpu.VMEM((64, 128), F32)] * 2, in_spe...  33.2 us

profile of v5, /device:TPU:32, one launch (start us, length us, event | category | flops | bytes accessed | tf_op | source)
XLA Modules:
  0.0 34.5 jit_solution(2276715462111398150)
XLA Ops:
  0.6 33.2 %shard_map.50 = (f32[64,128]{1,0:T(8,128)S(1)}, f32[64,128]{1,0:T(8,128)S(1)}) custom-call(f32[64,128]{1,0:T(8,128)} %bitcast.7, bf16[8,8,2,64,128]{4,3,2,1,0:T(8,128)(2,1)} %bitcast.5, bf16[8,2,64,128]{3,2,1,0:T(8,128)(2,1)} %bitcast.6), custom_call_target="tpu_custom_call" | custom-call | flops 10485760 | bytes 2621440 | tf_op jit(solution)/shard_map/pallas_call | solution.py:481
  33.9 0.6 %shard_map.51 = (f32[64,128]{1,0:T(8,128)}, f32[64,128]{1,0:T(8,128)}) custom-call(f32[64,128]{1,0:T(8,128)S(1)} %get-tuple-element.6.source, f32[64,128]{1,0:T(8,128)S(1)} %get-tuple-element.7.initial), custom_call_target="tpu_custom_call" | custom-call | tf_op jit(solution)/shard_map/pallas_call | solution.py:525

commit v6 on v5

--- a/solution.py
+++ b/solution.py
@@ -225,12 +225,6 @@
 
     for k in range(9):
         edge_b[1, k] = picked[k].astype(BF16)
-    towards, level, away = SLOTS[1]
-    out_b[1, 0] = pair_high(towards[0], towards[1]).astype(BF16)
-    out_b[1, 1] = pair_high(towards[2], 8).astype(BF16)
-    out_b[1, 2] = pair_high(*level).astype(BF16)
-    out_b[1, 3] = three(away, 4).astype(BF16)
-
     def along(src, dst, slot, way):
         return pltpu.make_async_remote_copy(
             src_ref=src,
@@ -326,6 +320,13 @@
         start(lambda way, step=step: [rows_copy(step, way)])
         if step == 0:
             start(lambda way: [blocks_copy(way)])
+            for k in range(9):
+                picked[k] = edge_b[1, k].astype(F32)
+            towards, level, away = SLOTS[1]
+            out_b[1, 0] = pair_high(towards[0], towards[1]).astype(BF16)
+            out_b[1, 1] = pair_high(towards[2], 8).astype(BF16)
+            out_b[1, 2] = pair_high(*level).astype(BF16)
+            out_b[1, 3] = three(away, 4).astype(BF16)
         if step < STEPS - 1:
             edge_w[1, step] = edges_of(w, 2)
         if step == STEPS - 2:

time: 34.7 us -> 34.7 us (level)
  no operation moved by 1% of the time
where the time goes in v6:
time: 34.7 us; the launch traced here: 34.5 us
  Pallas kernels  33.9 us (98%)
  between operations  0.64 us (2%)
    pallas_call x1, Pallas kernels, per_device(): pl.pallas_call(kernel, out_shape=[pltpu.VMEM((64, 128), F32)] * 2, in_spe...  33.2 us

profile of v6, /device:TPU:32, one launch (start us, length us, event | category | flops | bytes accessed | tf_op | source)
XLA Modules:
  0.0 34.5 jit_solution(13176190047625654553)
XLA Ops:
  0.6 33.2 %shard_map.50 = (f32[64,128]{1,0:T(8,128)S(1)}, f32[64,128]{1,0:T(8,128)S(1)}) custom-call(f32[64,128]{1,0:T(8,128)} %bitcast.7, bf16[8,8,2,64,128]{4,3,2,1,0:T(8,128)(2,1)} %bitcast.5, bf16[8,2,64,128]{3,2,1,0:T(8,128)(2,1)} %bitcast.6), custom_call_target="tpu_custom_call" | custom-call | flops 10485760 | bytes 2621440 | tf_op jit(solution)/shard_map/pallas_call | solution.py:482
  33.9 0.6 %shard_map.51 = (f32[64,128]{1,0:T(8,128)}, f32[64,128]{1,0:T(8,128)}) custom-call(f32[64,128]{1,0:T(8,128)S(1)} %get-tuple-element.6.source, f32[64,128]{1,0:T(8,128)S(1)} %get-tuple-element.7.initial), custom_call_target="tpu_custom_call" | custom-call | tf_op jit(solution)/shard_map/pallas_call | solution.py:526
